TPU v7x, 32 devices: a whole 2x2x4 slice. The times are simulated.
32 devices in a mesh: table: 8 (over y, x, core), batch: 4 (over z).
Axes of the slice: x: 2, y: 2, z: 4, core: 2. Of those that a mesh axis runs over, the one named last changes fastest.
Arguments:
- table_rows: float32 [192, 64, 128], P('table'), may hold values from -6 to 6
- accum: float32 [192, 64], P('table'), may hold values from 0.05 to 2
- plan_dest: int32 [8, 2], replicated, may hold values from 0 to 7, as said below
- plan_slot: int32 [8, 2], replicated, may hold values from 0 to 23, as said below
- bag_block: int32 [4096], P(('table', 'batch')), may hold values from 0 to 191, as said below
- bag_rows: int32 [4096, 8], P(('table', 'batch')), may hold values from 0 to 63
- grad_pooled: float32 [4096, 128], P(('table', 'batch')), may hold values from -6 to 6
Outputs:
- pooled: float32 [4096, 128], P(('table', 'batch'))
- table_new: float32 [192, 64, 128], P('table')
- accum_new: float32 [192, 64], P('table')
Inputs may be any that keep to these rules, and one draw needn't show every extreme that they name: `plan_dest`: row s names 2 distinct owners, none equal to s; every owner is named in exactly 2 rows. `plan_slot`: the slots of one row are distinct. `bag_block`: after migration, at most 64 samples of one device read blocks held by one owner; in every draw some owner is read by exactly 64 samples of every device.
All inputs are finite; a program needn't handle non-finite values.
Results may differ from a plain program's by a relative error of at most 0.00002.
Values sent between devices are 32-bit elements; how exact they have to be, the bound alone decides.
A program may use at most 64 MiB of HBM per device.

v0:
```python
import functools

import jax
import jax.numpy as jnp
from jax import lax
from jax.experimental import pallas as pl
from jax.experimental.pallas import tpu as pltpu
from jax.sharding import PartitionSpec as P

LEARN_RATE = 0.3
EPSILON = 1e-08
MESH = pl.DeviceIdType.MESH
EXACT = lax.Precision.HIGHEST


def split_halves(values):
    high = values.astype(jnp.bfloat16)
    low = (values - high.astype(jnp.float32)).astype(jnp.bfloat16)
    return jnp.concatenate([high, low], axis=1)


def kernel(
    n, reps, cap,
    picked, source, bucket_row, bucket_col, lane_col, rows_t, table, accum, grad,
    pooled_out, table_out, accum_out,
    comb, mig_send, ids_send, grad_send, grads, ids, moved_hl, total, pool_part, pool_back,
    send_sem, recv_sem, zsend_sem, zrecv_sem, psend_sem, precv_sem,
):
    me = lax.axis_index("table")
    rep = lax.axis_index("batch")
    blocks, brows, dim = table.shape
    samples = grad.shape[0]
    slots = n * cap
    groups = slots // 128
    per_group = 128 // cap
    has_up = rep < reps - 1
    has_down = rep > 0
    step_blocks = 4 if blocks % 4 == 0 else 1

    barrier = pltpu.get_barrier_semaphore()
    for d in range(1, n):
        pl.semaphore_signal(
            barrier, inc=1, device_id={"table": lax.rem(me + d, n)}, device_id_type=MESH
        )

    @pl.when(has_up)
    def _():
        pl.semaphore_signal(barrier, inc=1, device_id={"batch": rep + 1}, device_id_type=MESH)

    @pl.when(has_down)
    def _():
        pl.semaphore_signal(barrier, inc=1, device_id={"batch": rep - 1}, device_id_type=MESH)

    place = (
        lax.broadcasted_iota(jnp.int32, (slots, samples), 0) == bucket_row[...]
    ).astype(jnp.float32)
    sent = jnp.dot(place, grad[...], precision=EXACT, preferred_element_type=jnp.float32)
    grad_send[...] = sent.reshape(n, cap, dim)
    lanes = (
        lax.broadcasted_iota(jnp.int32, (samples, n * 128), 1) == lane_col[...]
    ).astype(jnp.float32)
    sent_ids = jnp.dot(rows_t[...], lanes, precision=EXACT, preferred_element_type=jnp.float32)
    for d in range(n):
        ids_send[d] = sent_ids[:, d * 128 : (d + 1) * 128]

    for d in range(n):
        mig_send[d, 0:brows, :] = table[picked[d]]
        mig_send[d, brows:, :] = jnp.zeros((8, dim), jnp.float32)
        mig_send[d, brows : brows + 1, 0:brows] = accum[pl.ds(picked[d], 1), :]

    neighbours = jnp.where(has_up, 1, 0) + jnp.where(has_down, 1, 0)
    pl.semaphore_wait(barrier, n - 1 + neighbours)

    def exchange(kind, src, dst, peer):
        return pltpu.make_async_remote_copy(
            src_ref=src, dst_ref=dst,
            send_sem=send_sem.at[kind, peer], recv_sem=recv_sem.at[kind, me],
            device_id={"table": peer}, device_id_type=MESH,
        )

    def arrival(kind, dst, peer):
        return pltpu.make_async_remote_copy(
            src_ref=dst, dst_ref=dst,
            send_sem=send_sem.at[kind, peer], recv_sem=recv_sem.at[kind, peer],
            device_id={"table": peer}, device_id_type=MESH,
        )

    peers = [lax.rem(me + d, n) for d in range(1, n)]
    for peer in peers:
        exchange(0, ids_send.at[peer], ids.at[rep, me], peer).start()
        exchange(1, grad_send.at[peer], grads.at[rep, me], peer).start()
    for peer in peers:
        exchange(2, mig_send.at[peer], comb.at[blocks + me], peer).start()
    ids[rep, me] = ids_send[me]
    grads[rep, me] = grad_send[me]

    comb[0:blocks, 0:brows, :] = table[...]
    comb[0:blocks, brows:, :] = jnp.zeros((blocks, 8, dim), jnp.float32)
    comb[blocks + me] = jnp.zeros((brows + 8, dim), jnp.float32)
    for j in range(blocks):
        comb[j, brows : brows + 1, 0:brows] = accum[j : j + 1, :]

    for peer in peers:
        arrival(0, ids.at[rep, peer], peer).wait_recv()
        arrival(1, grads.at[rep, peer], peer).wait_recv()

    def hop(kind, way, origin):
        buffer = ids if kind == 0 else grads
        return pltpu.make_async_remote_copy(
            src_ref=buffer.at[origin], dst_ref=buffer.at[origin],
            send_sem=zsend_sem.at[way, kind, origin], recv_sem=zrecv_sem.at[kind, origin],
            device_id={"batch": rep + 1 - 2 * way}, device_id_type=MESH,
        )

    def send_on(way, origin):
        for kind in range(2):
            hop(kind, way, origin).start()

    @pl.when(has_up)
    def _():
        send_on(0, rep)

    @pl.when(has_down)
    def _():
        send_on(1, rep)

    for peer in peers:
        arrival(2, comb.at[blocks + peer], peer).wait_recv()

    row_id = lax.broadcasted_iota(jnp.int32, (brows, 128), 0)

    def counts_of(origin):
        places, counts = [], []
        for g in range(groups):
            named = ids[origin, g * per_group]
            for s in range(1, per_group):
                named = named + ids[origin, g * per_group + s]
            named = named.astype(jnp.int32) - 1
            places.append(jnp.right_shift(named[0:1, :], (brows - 1).bit_length()))
            rows = jnp.bitwise_and(named, brows - 1)
            count = jnp.zeros((brows, 128), jnp.float32)
            for k in range(rows.shape[0]):
                count = count + (rows[k : k + 1, :] == row_id).astype(jnp.float32)
            counts.append(count)
        return jnp.concatenate(places, axis=1), jnp.concatenate(counts, axis=1)

    def chosen(places, counts, first):
        return jnp.concatenate(
            [
                jnp.where(places == first + b, counts, 0.0).astype(jnp.bfloat16)
                for b in range(step_blocks)
            ],
            axis=0,
        )

    span = step_blocks * brows

    def copy_moved(j, carry):
        moved_hl[pl.ds(pl.multiple_of(j * brows, brows), brows), :] = split_halves(
            comb[source[j], 0:brows, :]
        )
        return carry

    lax.fori_loop(0, blocks, copy_moved, 0)

    pool_part[...] = jnp.zeros_like(pool_part)
    places, counts = counts_of(rep)
    gradients = split_halves(grads[rep].reshape(slots, dim))

    def own_step(i, carry):
        hits = chosen(places, counts, i * step_blocks)
        where = pl.ds(pl.multiple_of(i * span, span), span)
        total[where, :] = jnp.dot(hits, gradients, preferred_element_type=jnp.float32)
        both = lax.dot_general(
            hits, moved_hl[where, :], (((0,), (0,)), ((), ())),
            preferred_element_type=jnp.float32,
        )
        pool_part[...] += (both[:, :dim] + both[:, dim:]).reshape(n, cap, dim)
        return carry

    lax.fori_loop(0, blocks // step_blocks, own_step, 0)

    def give_back(peer):
        return pltpu.make_async_remote_copy(
            src_ref=pool_part.at[peer], dst_ref=pool_back.at[me],
            send_sem=psend_sem.at[peer], recv_sem=precv_sem.at[me],
            device_id={"table": peer}, device_id_type=MESH,
        )

    def given_back(peer):
        return pltpu.make_async_remote_copy(
            src_ref=pool_part.at[peer], dst_ref=pool_back.at[peer],
            send_sem=psend_sem.at[peer], recv_sem=precv_sem.at[peer],
            device_id={"table": peer}, device_id_type=MESH,
        )

    for peer in peers:
        give_back(peer).start()
    pool_back[me] = pool_part[me]

    def add_origin(origin):
        places, counts = counts_of(origin)
        gradients = split_halves(grads[origin].reshape(slots, dim))

        def step(i, carry):
            hits = chosen(places, counts, i * step_blocks)
            where = pl.ds(pl.multiple_of(i * span, span), span)
            total[where, :] += jnp.dot(hits, gradients, preferred_element_type=jnp.float32)
            return carry

        lax.fori_loop(0, blocks // step_blocks, step, 0)

    def far_step(h, carry):
        below = rep - h
        above = rep + h

        @pl.when(below >= 0)
        def _():
            for kind in range(2):
                hop(kind, 0, below).wait_recv()

            @pl.when(has_up)
            def _():
                send_on(0, below)

        @pl.when(above < reps)
        def _():
            for kind in range(2):
                hop(kind, 1, above).wait_recv()

            @pl.when(has_down)
            def _():
                send_on(1, above)

        @pl.when(below >= 0)
        def _():
            add_origin(below)

        @pl.when(above < reps)
        def _():
            add_origin(above)

        return carry

    lax.fori_loop(1, reps, far_step, 0)

    eye = lax.broadcasted_iota(jnp.int32, (brows, brows), 0) == lax.broadcasted_iota(
        jnp.int32, (brows, brows), 1
    )

    def update(j, carry):
        where = pl.ds(pl.multiple_of(j * brows, brows), brows)
        both = total[where, :]
        row_grad = both[:, :dim] + both[:, dim:]
        at = source[j]
        old = comb[at, brows : brows + 1, 0:brows]
        old = jnp.sum(jnp.where(eye, old, 0.0), axis=1, keepdims=True)
        new = old + jnp.mean(row_grad * row_grad, axis=1, keepdims=True)
        table_out[j] = comb[at, 0:brows, :] - (LEARN_RATE * row_grad) / (jnp.sqrt(new) + EPSILON)
        accum_out[pl.ds(j, 1), :] = jnp.sum(jnp.where(eye, new, 0.0), axis=0, keepdims=True)
        return carry

    lax.fori_loop(0, blocks, update, 0)

    for peer in peers:
        given_back(peer).wait_recv()
    back = (
        lax.broadcasted_iota(jnp.int32, (samples, slots), 1) == bucket_col[...]
    ).astype(jnp.float32)
    pooled_out[...] = jnp.dot(
        back, pool_back[...].reshape(slots, dim), precision=EXACT,
        preferred_element_type=jnp.float32,
    )

    for peer in peers:
        exchange(0, ids_send.at[peer], ids.at[rep, me], peer).wait_send()
        exchange(1, grad_send.at[peer], grads.at[rep, me], peer).wait_send()
        exchange(2, mig_send.at[peer], comb.at[blocks + me], peer).wait_send()
        give_back(peer).wait_send()

    def drain(origin, carry):
        @pl.when(jnp.logical_and(has_up, origin <= rep))
        def _():
            for kind in range(2):
                hop(kind, 0, origin).wait_send()

        @pl.when(jnp.logical_and(has_down, origin >= rep))
        def _():
            for kind in range(2):
                hop(kind, 1, origin).wait_send()

        return carry

    lax.fori_loop(0, reps, drain, 0)


def per_device(table_rows, accum, plan_dest, plan_slot, bag_block, bag_rows, grad_pooled):
    blocks, brows, dim = table_rows.shape
    n = lax.axis_size("table")
    reps = lax.axis_size("batch")
    me = lax.axis_index("table")
    moving = plan_dest.shape[1]
    samples, pool = bag_rows.shape
    cap = 4 * samples // n
    owners = jnp.arange(n, dtype=jnp.int32)

    targets = plan_dest.reshape(-1)
    sources = jnp.arange(n * moving, dtype=jnp.int32) // moving
    earlier = (targets[:, None] == targets[None, :]) & (sources[None, :] < sources[:, None])
    rank = jnp.sum(earlier.astype(jnp.int32), axis=1)
    landing_at = targets * moving + rank
    every = jnp.arange(n * moving, dtype=jnp.int32)
    landing = jnp.sum(
        jnp.where(landing_at[:, None] == every[None, :], plan_slot.reshape(-1)[None, :], 0), axis=1
    )
    old_spot = sources * blocks + plan_slot.reshape(-1)
    new_spot = targets * blocks + landing

    mine = sources == me
    picked = jnp.sum(
        jnp.where(
            mine[None, :] & (targets[None, :] == owners[:, None]), plan_slot.reshape(-1)[None, :], 0
        ),
        axis=1,
    )
    spots = me * blocks + jnp.arange(blocks, dtype=jnp.int32)
    comes = new_spot[None, :] == spots[:, None]
    source = jnp.where(
        jnp.any(comes, axis=1),
        blocks + jnp.sum(jnp.where(comes, sources[None, :], 0), axis=1),
        jnp.arange(blocks, dtype=jnp.int32),
    )

    moves = bag_block[:, None] == old_spot[None, :]
    read = bag_block + jnp.sum(jnp.where(moves, (new_spot - old_spot)[None, :], 0), axis=1)
    owner = read // blocks
    order = jnp.arange(samples, dtype=jnp.int32)
    slot = jnp.sum(
        ((owner[:, None] == owner[None, :]) & (order[None, :] < order[:, None])).astype(jnp.int32),
        axis=1,
    )
    bucket = owner * cap + slot
    lane = owner * 128 + (me % (128 // cap)) * cap + slot
    rows_t = (((read - owner * blocks) * brows)[None, :] + bag_rows.T + 1).astype(jnp.float32)

    vmem = pl.BlockSpec(memory_space=pltpu.VMEM)
    smem = pl.BlockSpec(memory_space=pltpu.SMEM)
    slots = n * cap
    f32 = jnp.float32
    return pl.pallas_call(
        functools.partial(kernel, n, reps, cap),
        out_shape=(
            jax.ShapeDtypeStruct((samples, dim), f32),
            jax.ShapeDtypeStruct((blocks, brows, dim), f32),
            jax.ShapeDtypeStruct((blocks, brows), f32),
        ),
        in_specs=[smem] * 2 + [vmem] * 7,
        out_specs=(vmem, vmem, vmem),
        scratch_shapes=[
            pltpu.VMEM((blocks + n, brows + 8, dim), f32),
            pltpu.VMEM((n, brows + 8, dim), f32),
            pltpu.VMEM((n, pool, 128), f32),
            pltpu.VMEM((n, cap, dim), f32),
            pltpu.VMEM((reps, n, cap, dim), f32),
            pltpu.VMEM((reps, n, pool, 128), f32),
            pltpu.VMEM((blocks * brows, 2 * dim), jnp.bfloat16),
            pltpu.VMEM((blocks * brows, 2 * dim), f32),
            pltpu.VMEM((n, cap, dim), f32),
            pltpu.VMEM((n, cap, dim), f32),
            pltpu.SemaphoreType.DMA((3, n)),
            pltpu.SemaphoreType.DMA((3, n)),
            pltpu.SemaphoreType.DMA((2, 2, reps)),
            pltpu.SemaphoreType.DMA((2, reps)),
            pltpu.SemaphoreType.DMA((n,)),
            pltpu.SemaphoreType.DMA((n,)),
        ],
        compiler_params=pltpu.CompilerParams(
            collective_id=0, has_side_effects=True, vmem_limit_bytes=48 * 1024 * 1024
        ),
    )(
        picked, source, bucket[None, :], bucket[:, None], lane[:, None], rows_t,
        table_rows, accum, grad_pooled,
    )


def solution(mesh):
    return jax.shard_map(
        per_device,
        mesh=mesh,
        in_specs=(
            P("table", None, None),
            P("table", None),
            P(),
            P(),
            P(("table", "batch")),
            P(("table", "batch"), None),
            P(("table", "batch"), None),
        ),
        out_specs=(P(("table", "batch"), None), P("table", None, None), P("table", None)),
        check_vma=False,
    )
```

profile of v0, /device:TPU:0, one launch (start us, length us, event | category | flops | bytes accessed | tf_op | source)
XLA Modules:
  0.0 50.5 jit_solution(6727002195595302805)
XLA Ops:
  0.7 0.7 %copy-done.5 = s32[8,2]{0,1:T(2,128)S(1)} copy-done((s32[8,2]{0,1:T(2,128)S(1)}, s32[8,2]{0,1:T(2,128)}, u32[]{:S(2)}) %copy-start.5) | copy-done | bytes 88
  1.4 0.1 copy.18
  1.4 0.1 eq.94
  1.5 0.2 convert_reduce_fusion.1
  1.7 0.7 %copy-done.6 = s32[8,2]{0,1:T(2,128)S(1)} copy-done((s32[8,2]{0,1:T(2,128)S(1)}, s32[8,2]{0,1:T(2,128)}, u32[]{:S(2)}) %copy-start.6) | copy-done | bytes 88
  2.4 0.1 copy.19
  2.5 0.1 broadcast_in_dim.76
  2.5 0.2 select_reduce_fusion.1
  2.7 0.1 select_reduce_fusion.2.picked
  2.9 0.1 fusion.1
  3.0 0.1 compare_reduce_fusion
  3.0 0.0 copy-start.4
  3.1 0.6 %copy-done.4 = s32[128]{0:T(128)S(1)} copy-done((s32[128]{0:T(128)S(1)}, s32[128]{0:T(128)}, u32[]{:S(2)}) %copy-start.4) | copy-done | bytes 536
  3.7 0.1 select_reduce_fusion
  3.8 0.2 convert_reduce_fusion
  4.0 0.7 %copy-done.3 = s32[128,8]{0,1:T(8,128)S(1)} copy-done((s32[128,8]{0,1:T(8,128)S(1)}, s32[128,8]{0,1:T(8,128)}, u32[]{:S(2)}) %copy-start.3) | copy-done | bytes 4120
  4.7 0.1 copy.21.lane_col
  4.8 0.1 copy.20.bucket_col
  4.9 0.6 %copy-done.1 = f32[128,128]{1,0:T(8,128)S(1)} copy-done((f32[128,128]{1,0:T(8,128)S(1)}, f32[128,128]{1,0:T(8,128)}, u32[]{:S(2)}) %copy-start.1) | copy-done | bytes 65560
  5.5 1.1 %copy-done = f32[24,64,128]{2,1,0:T(8,128)S(1)} copy-done((f32[24,64,128]{2,1,0:T(8,128)S(1)}, f32[24,64,128]{2,1,0:T(8,128)}, u32[]{:S(2)}) %copy-start) | copy-done | bytes 786456
  6.7 41.7 %shard_map.94 = (f32[128,128]{1,0:T(8,128)S(1)}, f32[24,64,128]{2,1,0:T(8,128)S(1)}, f32[24,64]{1,0:T(8,128)S(1)}) custom-call(s32[8]{0:T(128)S(1)} %select_reduce_fusion.2.picked, s32[24]{0:T(128)S(1)} %iota_select_fusion.source, s32[1,128]{1,0:T(1,128)S(1)} %get-tuple-element.9.bucket_row, s32[128,1]{1,0:T(8,128)S(1)} %copy.20.bucket_col, ...), custom_call_target="tpu_custom_call" | custom-call | tf_op jit(solution)/shard_map/pallas_call | solution.py:350
  48.4 0.6 %copy.25 = f32[128,128]{1,0:T(8,128)} copy(f32[128,128]{1,0:T(8,128)S(1)} %get-tuple-element.14) | data formatting | bytes 131072
  49.0 0.9 %copy.26 = f32[24,64,128]{2,1,0:T(8,128)} copy(f32[24,64,128]{2,1,0:T(8,128)S(1)} %get-tuple-element.15) | data formatting | bytes 1572864
  49.9 0.6 %copy.27 = f32[24,64]{1,0:T(8,128)} copy(f32[24,64]{1,0:T(8,128)S(1)} %get-tuple-element.16) | data formatting | bytes 12288
  (16 shorter events, 0.1 us)
Async XLA Ops:
  0.7 0.7 %copy-start.5 = (s32[8,2]{0,1:T(2,128)S(1)}, s32[8,2]{0,1:T(2,128)}, u32[]{:S(2)}) copy-start(s32[8,2]{0,1:T(2,128)} %param.9) | copy-start | bytes 196
  1.7 0.7 %copy-start.6 = (s32[8,2]{0,1:T(2,128)S(1)}, s32[8,2]{0,1:T(2,128)}, u32[]{:S(2)}) copy-start(s32[8,2]{0,1:T(2,128)} %param.10) | copy-start | bytes 196
  3.0 0.7 %copy-start.4 = (s32[128]{0:T(128)S(1)}, s32[128]{0:T(128)}, u32[]{:S(2)}) copy-start(s32[128]{0:T(128)} %param.11) | copy-start | bytes 1540
  4.0 0.7 %copy-start.3 = (s32[128,8]{0,1:T(8,128)S(1)}, s32[128,8]{0,1:T(8,128)}, u32[]{:S(2)}) copy-start(s32[128,8]{0,1:T(8,128)} %param.12) | copy-start | bytes 12292
  4.7 0.8 %copy-start.1 = (f32[128,128]{1,0:T(8,128)S(1)}, f32[128,128]{1,0:T(8,128)}, u32[]{:S(2)}) copy-start(f32[128,128]{1,0:T(8,128)} %grad.1) | copy-start | bytes 196612
  4.8 0.7 %copy-start.2 = (f32[24,64]{1,0:T(8,128)S(1)}, f32[24,64]{1,0:T(8,128)}, u32[]{:S(2)}) copy-start(f32[24,64]{1,0:T(8,128)} %accum.1) | copy-start | bytes 18436
  5.5 1.1 %copy-start = (f32[24,64,128]{2,1,0:T(8,128)S(1)}, f32[24,64,128]{2,1,0:T(8,128)}, u32[]{:S(2)}) copy-start(f32[24,64,128]{2,1,0:T(8,128)} %table.1) | copy-start | bytes 2359300
where the time goes:
time: 50.8 us; the launch traced here: 50.5 us
  Pallas kernels  41.7 us (82%)
  local copies, waits for them, and re-layouts  7.06 us (14%)
  other arithmetic  0.98 us (2%)
  between operations  0.75 us (1%)
    pallas_call x1, Pallas kernels, per_device(): pl.pallas_call(functools.partial(kernel, n, reps, cap), out_shape=(jax.Sh...  41.7 us
    unnamed x19, local copies, waits for them, and re-layouts  6.67 us

commit v1 on v0

--- a/solution.py
+++ b/solution.py
@@ -19,7 +19,7 @@
     return jnp.concatenate([high, low], axis=1)
 
 
-def kernel(
+def bucket_kernel(
     n, reps, cap,
     picked, source, bucket_row, bucket_col, lane_col, rows_t, table, accum, grad,
     pooled_out, table_out, accum_out,
@@ -294,6 +294,300 @@
     lax.fori_loop(0, reps, drain, 0)
 
 
+def gather_kernel(
+    n, reps, cap,
+    picked, source, bucket_col, lane_col, rows_t, named_t, table, accum, grad,
+    pooled_out, table_out, accum_out,
+    comb, mig_send, ids_send, units, ids, moved_hl, total, pool_part, pool_back,
+    send_sem, recv_sem, zsend_sem, zrecv_sem, usend_sem, urecv_sem, psend_sem, precv_sem,
+):
+    me = lax.axis_index("table")
+    rep = lax.axis_index("batch")
+    blocks, brows, dim = table.shape
+    samples = grad.shape[0]
+    slots = n * cap
+    groups = slots // 128
+    per_group = 128 // cap
+    has_up = rep < reps - 1
+    has_down = rep > 0
+    step_blocks = 4 if blocks % 4 == 0 else 1
+    span = step_blocks * brows
+
+    barrier = pltpu.get_barrier_semaphore()
+    for d in range(1, n):
+        pl.semaphore_signal(
+            barrier, inc=1, device_id={"table": lax.rem(me + d, n)}, device_id_type=MESH
+        )
+
+    @pl.when(has_up)
+    def _():
+        pl.semaphore_signal(barrier, inc=1, device_id={"batch": rep + 1}, device_id_type=MESH)
+
+    @pl.when(has_down)
+    def _():
+        pl.semaphore_signal(barrier, inc=1, device_id={"batch": rep - 1}, device_id_type=MESH)
+
+    units[rep, me, 0:samples, :] = grad[...]
+    units[rep, me, samples:, :] = named_t[...]
+    lanes = (
+        lax.broadcasted_iota(jnp.int32, (samples, n * 128), 1) == lane_col[...]
+    ).astype(jnp.float32)
+    sent_ids = jnp.dot(rows_t[...], lanes, precision=EXACT, preferred_element_type=jnp.float32)
+    for d in range(n):
+        ids_send[d] = sent_ids[:, d * 128 : (d + 1) * 128]
+        mig_send[d, 0:brows, :] = table[picked[d]]
+        mig_send[d, brows:, :] = jnp.zeros((8, dim), jnp.float32)
+        mig_send[d, brows : brows + 1, 0:brows] = accum[pl.ds(picked[d], 1), :]
+
+    neighbours = jnp.where(has_up, 1, 0) + jnp.where(has_down, 1, 0)
+    pl.semaphore_wait(barrier, n - 1 + neighbours)
+
+    def exchange(kind, src, dst, peer):
+        return pltpu.make_async_remote_copy(
+            src_ref=src, dst_ref=dst,
+            send_sem=send_sem.at[kind, peer], recv_sem=recv_sem.at[kind, me],
+            device_id={"table": peer}, device_id_type=MESH,
+        )
+
+    def arrival(kind, dst, peer):
+        return pltpu.make_async_remote_copy(
+            src_ref=dst, dst_ref=dst,
+            send_sem=send_sem.at[kind, peer], recv_sem=recv_sem.at[kind, peer],
+            device_id={"table": peer}, device_id_type=MESH,
+        )
+
+    peers = [lax.rem(me + d, n) for d in range(1, n)]
+
+    parity = me % 2
+    across = me + 4 - 8 * ((me // 4) % 2)
+    along = me + 2 - 4 * ((me // 2) % 2)
+    first = across + parity * (along - across)
+    second = along + parity * (across - along)
+    beside = me + 1 - 2 * parity
+    corner = first + second - me
+
+    def hop(way, origin):
+        return pltpu.make_async_remote_copy(
+            src_ref=units.at[origin, me], dst_ref=units.at[origin, me],
+            send_sem=zsend_sem.at[way, origin], recv_sem=zrecv_sem.at[origin],
+            device_id={"batch": rep + 1 - 2 * way}, device_id_type=MESH,
+        )
+
+    def relay(stage, origin, unit):
+        return pltpu.make_async_remote_copy(
+            src_ref=units.at[origin, unit], dst_ref=units.at[origin, unit],
+            send_sem=usend_sem.at[stage, origin, unit], recv_sem=urecv_sem.at[origin, unit],
+            device_id={"table": (first, second, beside)[stage]}, device_id_type=MESH,
+        )
+
+    def over(step, body):
+        if step == 0:
+            body(rep, None)
+            return
+
+        @pl.when(rep - step >= 0)
+        def _():
+            body(rep - step, 0)
+
+        @pl.when(rep + step < reps)
+        def _():
+            body(rep + step, 1)
+
+    def enter(origin, way):
+        if way is not None:
+            hop(way, origin).wait_recv()
+        if way != 1:
+            @pl.when(has_up)
+            def _():
+                hop(0, origin).start()
+        if way != 0:
+            @pl.when(has_down)
+            def _():
+                hop(1, origin).start()
+        for stage in range(3):
+            relay(stage, origin, me).start()
+
+    def from_first(origin, way):
+        relay(0, origin, first).wait_recv()
+        relay(1, origin, first).start()
+        relay(2, origin, first).start()
+
+    def from_second(origin, way):
+        for unit in (second, corner):
+            relay(1, origin, unit).wait_recv()
+            relay(2, origin, unit).start()
+
+    row_id = lax.broadcasted_iota(jnp.int32, (brows, 128), 0)
+
+    def count_rows(named):
+        rows = jnp.bitwise_and(named, brows - 1)
+        count = jnp.zeros((brows, 128), jnp.float32)
+        for k in range(rows.shape[0]):
+            count = count + (rows[k : k + 1, :] == row_id).astype(jnp.float32)
+        return jnp.right_shift(named[0:1, :], (brows - 1).bit_length()), count
+
+    def chosen(places, counts, start):
+        return jnp.concatenate(
+            [
+                jnp.where(places == start + b, counts, 0.0).astype(jnp.bfloat16)
+                for b in range(step_blocks)
+            ],
+            axis=0,
+        )
+
+    def joined(pairs):
+        return (
+            jnp.concatenate([p for p, _ in pairs], axis=1),
+            jnp.concatenate([c for _, c in pairs], axis=1),
+        )
+
+    def add_units(origin, which):
+        places, counts = joined(
+            [
+                count_rows(units[origin, u, samples:, :].astype(jnp.int32) - me * (blocks * brows))
+                for u in which
+            ]
+        )
+        gradients = jnp.concatenate(
+            [split_halves(units[origin, u, 0:samples, :]) for u in which], axis=0
+        )
+
+        def step(i, carry):
+            hits = chosen(places, counts, i * step_blocks)
+            where = pl.ds(pl.multiple_of(i * span, span), span)
+            total[where, :] += jnp.dot(hits, gradients, preferred_element_type=jnp.float32)
+            return carry
+
+        lax.fori_loop(0, blocks // step_blocks, step, 0)
+
+    def finish_near(origin, way):
+        add_units(origin, (me, first, second, corner))
+
+    beyond = [u + 1 - 2 * parity for u in (me, first, second, corner)]
+
+    def finish_far(origin, way):
+        for unit in beyond:
+            relay(2, origin, unit).wait_recv()
+        add_units(origin, beyond)
+
+    over(0, enter)
+    for peer in peers:
+        exchange(0, ids_send.at[peer], ids.at[me], peer).start()
+    for peer in peers:
+        exchange(1, mig_send.at[peer], comb.at[blocks + me], peer).start()
+    ids[me] = ids_send[me]
+    comb[0:blocks, 0:brows, :] = table[...]
+    comb[0:blocks, brows:, :] = jnp.zeros((blocks, 8, dim), jnp.float32)
+    comb[blocks + me] = jnp.zeros((brows + 8, dim), jnp.float32)
+    for j in range(blocks):
+        comb[j, brows : brows + 1, 0:brows] = accum[j : j + 1, :]
+    total[...] = jnp.zeros_like(total)
+    pool_part[...] = jnp.zeros_like(pool_part)
+
+    if reps > 1:
+        over(1, enter)
+    over(0, from_first)
+
+    for peer in peers:
+        arrival(0, ids.at[peer], peer).wait_recv()
+    for peer in peers:
+        arrival(1, comb.at[blocks + peer], peer).wait_recv()
+    pairs = []
+    for g in range(groups):
+        named = ids[g * per_group]
+        for s in range(1, per_group):
+            named = named + ids[g * per_group + s]
+        pairs.append(count_rows(named.astype(jnp.int32) - 1))
+    asked, asked_counts = joined(pairs)
+
+    def copy_moved(j, carry):
+        moved_hl[pl.ds(pl.multiple_of(j * brows, brows), brows), :] = split_halves(
+            comb[source[j], 0:brows, :]
+        )
+        return carry
+
+    lax.fori_loop(0, blocks, copy_moved, 0)
+
+    def pool_step(i, carry):
+        where = pl.ds(pl.multiple_of(i * span, span), span)
+        both = lax.dot_general(
+            chosen(asked, asked_counts, i * step_blocks), moved_hl[where, :],
+            (((0,), (0,)), ((), ())), preferred_element_type=jnp.float32,
+        )
+        pool_part[...] += (both[:, :dim] + both[:, dim:]).reshape(n, cap, dim)
+        return carry
+
+    lax.fori_loop(0, blocks // step_blocks, pool_step, 0)
+
+    def give_back(peer, owner):
+        return pltpu.make_async_remote_copy(
+            src_ref=pool_part.at[peer], dst_ref=pool_back.at[owner],
+            send_sem=psend_sem.at[peer], recv_sem=precv_sem.at[owner],
+            device_id={"table": peer}, device_id_type=MESH,
+        )
+
+    for peer in peers:
+        give_back(peer, me).start()
+    pool_back[me] = pool_part[me]
+
+    for step in range(2, reps + 4):
+        for lag, body in ((0, enter), (1, from_first), (2, from_second)):
+            if 0 <= step - lag < reps:
+                over(step - lag, body)
+        for lag, body in ((2, finish_near), (3, finish_far)):
+            if 0 <= step - lag < reps:
+                over(step - lag, body)
+
+    eye = lax.broadcasted_iota(jnp.int32, (brows, brows), 0) == lax.broadcasted_iota(
+        jnp.int32, (brows, brows), 1
+    )
+
+    def update(j, carry):
+        where = pl.ds(pl.multiple_of(j * brows, brows), brows)
+        both = total[where, :]
+        row_grad = both[:, :dim] + both[:, dim:]
+        at = source[j]
+        old = comb[at, brows : brows + 1, 0:brows]
+        old = jnp.sum(jnp.where(eye, old, 0.0), axis=1, keepdims=True)
+        new = old + jnp.mean(row_grad * row_grad, axis=1, keepdims=True)
+        table_out[j] = comb[at, 0:brows, :] - (LEARN_RATE * row_grad) / (jnp.sqrt(new) + EPSILON)
+        accum_out[pl.ds(j, 1), :] = jnp.sum(jnp.where(eye, new, 0.0), axis=0, keepdims=True)
+        return carry
+
+    lax.fori_loop(0, blocks, update, 0)
+
+    for peer in peers:
+        give_back(peer, peer).wait_recv()
+    back = (
+        lax.broadcasted_iota(jnp.int32, (samples, slots), 1) == bucket_col[...]
+    ).astype(jnp.float32)
+    pooled_out[...] = jnp.dot(
+        back, pool_back[...].reshape(slots, dim), precision=EXACT,
+        preferred_element_type=jnp.float32,
+    )
+
+    for peer in peers:
+        exchange(0, ids_send.at[peer], ids.at[me], peer).wait_send()
+        exchange(1, mig_send.at[peer], comb.at[blocks + me], peer).wait_send()
+        give_back(peer, me).wait_send()
+
+    def drain(origin, carry):
+        @pl.when(jnp.logical_and(has_up, origin <= rep))
+        def _():
+            hop(0, origin).wait_send()
+
+        @pl.when(jnp.logical_and(has_down, origin >= rep))
+        def _():
+            hop(1, origin).wait_send()
+
+        for stage, sent in ((0, (me,)), (1, (me, first)), (2, (me, first, second, corner))):
+            for unit in sent:
+                relay(stage, origin, unit).wait_send()
+        return carry
+
+    lax.fori_loop(0, reps, drain, 0)
+
+
 def per_device(table_rows, accum, plan_dest, plan_slot, bag_block, bag_rows, grad_pooled):
     blocks, brows, dim = table_rows.shape
     n = lax.axis_size("table")
@@ -347,13 +641,48 @@
     smem = pl.BlockSpec(memory_space=pltpu.SMEM)
     slots = n * cap
     f32 = jnp.float32
+    out_shape = (
+        jax.ShapeDtypeStruct((samples, dim), f32),
+        jax.ShapeDtypeStruct((blocks, brows, dim), f32),
+        jax.ShapeDtypeStruct((blocks, brows), f32),
+    )
+    unit_bytes = 4 * (samples + pool) * dim
+    if n == 8 and pool == 8 and samples == 128 and n * reps * unit_bytes <= 16 * 1024 * 1024:
+        named_t = ((read * brows)[None, :] + bag_rows.T).astype(f32)
+        return pl.pallas_call(
+            functools.partial(gather_kernel, n, reps, cap),
+            out_shape=out_shape,
+            in_specs=[smem] * 2 + [vmem] * 7,
+            out_specs=(vmem, vmem, vmem),
+            scratch_shapes=[
+                pltpu.VMEM((blocks + n, brows + 8, dim), f32),
+                pltpu.VMEM((n, brows + 8, dim), f32),
+                pltpu.VMEM((n, pool, 128), f32),
+                pltpu.VMEM((reps, n, samples + pool, dim), f32),
+                pltpu.VMEM((n, pool, 128), f32),
+                pltpu.VMEM((blocks * brows, 2 * dim), jnp.bfloat16),
+                pltpu.VMEM((blocks * brows, 2 * dim), f32),
+                pltpu.VMEM((n, cap, dim), f32),
+                pltpu.VMEM((n, cap, dim), f32),
+                pltpu.SemaphoreType.DMA((2, n)),
+                pltpu.SemaphoreType.DMA((2, n)),
+                pltpu.SemaphoreType.DMA((2, reps)),
+                pltpu.SemaphoreType.DMA((reps,)),
+                pltpu.SemaphoreType.DMA((3, reps, n)),
+                pltpu.SemaphoreType.DMA((reps, n)),
+                pltpu.SemaphoreType.DMA((n,)),
+                pltpu.SemaphoreType.DMA((n,)),
+            ],
+            compiler_params=pltpu.CompilerParams(
+                collective_id=1, has_side_effects=True, vmem_limit_bytes=48 * 1024 * 1024
+            ),
+        )(
+            picked, source, bucket[:, None], lane[:, None], rows_t, named_t,
+            table_rows, accum, grad_pooled,
+        )
     return pl.pallas_call(
-        functools.partial(kernel, n, reps, cap),
-        out_shape=(
-            jax.ShapeDtypeStruct((samples, dim), f32),
-            jax.ShapeDtypeStruct((blocks, brows, dim), f32),
-            jax.ShapeDtypeStruct((blocks, brows), f32),
-        ),
+        functools.partial(bucket_kernel, n, reps, cap),
+        out_shape=out_shape,
         in_specs=[smem] * 2 + [vmem] * 7,
         out_specs=(vmem, vmem, vmem),
         scratch_shapes=[

time: 50.8 us -> 46.6 us (0.917)
  Pallas kernels: 41.7 us -> 37.7 us
    pallas_call x1, Pallas kernels: 41.7 us -> 37.7 us  [per_device(): pl.pallas_call(functools.partial(gather_kernel, n, reps, cap), out_shape=...]
where the time goes in v1:
time: 46.6 us; the launch traced here: 46.3 us
  Pallas kernels  37.7 us (81%)
  local copies, waits for them, and re-layouts  6.87 us (15%)
  other arithmetic  0.99 us (2%)
  between operations  0.75 us (2%)
    pallas_call x1, Pallas kernels, per_device(): pl.pallas_call(functools.partial(gather_kernel, n, reps, cap), out_shape=...  37.7 us
    unnamed x19, local copies, waits for them, and re-layouts  6.49 us

profile of v1, /device:TPU:0, one launch (start us, length us, event | category | flops | bytes accessed | tf_op | source)
XLA Modules:
  0.0 46.3 jit_solution(203378200858528394)
XLA Ops:
  0.7 0.0 copy-start.5
  0.7 0.7 %copy-done.5 = s32[8,2]{0,1:T(2,128)S(1)} copy-done((s32[8,2]{0,1:T(2,128)S(1)}, s32[8,2]{0,1:T(2,128)}, u32[]{:S(2)}) %copy-start.5) | copy-done | bytes 88
  1.4 0.1 copy.18
  1.4 0.1 eq.94
  1.5 0.2 convert_reduce_fusion.1
  1.7 0.7 %copy-done.6 = s32[8,2]{0,1:T(2,128)S(1)} copy-done((s32[8,2]{0,1:T(2,128)S(1)}, s32[8,2]{0,1:T(2,128)}, u32[]{:S(2)}) %copy-start.6) | copy-done | bytes 88
  2.4 0.1 copy.19
  2.5 0.1 broadcast_in_dim.74
  2.5 0.2 select_reduce_fusion.1
  2.7 0.1 select_reduce_fusion.2.picked
  2.9 0.1 fusion.1
  3.0 0.1 compare_reduce_fusion
  3.1 0.6 %copy-done.4 = s32[128]{0:T(128)S(1)} copy-done((s32[128]{0:T(128)S(1)}, s32[128]{0:T(128)}, u32[]{:S(2)}) %copy-start.4) | copy-done | bytes 536
  3.7 0.1 select_reduce_fusion
  3.8 0.2 convert_reduce_fusion
  4.0 0.5 %copy-done.3 = s32[128,8]{0,1:T(8,128)S(1)} copy-done((s32[128,8]{0,1:T(8,128)S(1)}, s32[128,8]{0,1:T(8,128)}, u32[]{:S(2)}) %copy-start.3) | copy-done | bytes 4120
  4.5 0.1 copy.21.lane_col
  4.6 0.1 copy.20.bucket_col
  4.8 0.6 %copy-done.1 = f32[128,128]{1,0:T(8,128)S(1)} copy-done((f32[128,128]{1,0:T(8,128)S(1)}, f32[128,128]{1,0:T(8,128)}, u32[]{:S(2)}) %copy-start.1) | copy-done | bytes 65560
  5.4 1.1 %copy-done = f32[24,64,128]{2,1,0:T(8,128)S(1)} copy-done((f32[24,64,128]{2,1,0:T(8,128)S(1)}, f32[24,64,128]{2,1,0:T(8,128)}, u32[]{:S(2)}) %copy-start) | copy-done | bytes 786456
  6.5 37.7 %shard_map.94 = (f32[128,128]{1,0:T(8,128)S(1)}, f32[24,64,128]{2,1,0:T(8,128)S(1)}, f32[24,64]{1,0:T(8,128)S(1)}) custom-call(s32[8]{0:T(128)S(1)} %select_reduce_fusion.2.picked, s32[24]{0:T(128)S(1)} %iota_select_fusion.source, s32[128,1]{1,0:T(8,128)S(1)} %copy.20.bucket_col, s32[128,1]{1,0:T(8,128)S(1)} %copy.21.lane_col, ...), custom_call_target="tpu_custom_call" | custom-call | tf_op jit(solution)/shard_map/pallas_call | solution.py:652
  44.2 0.6 %copy.25 = f32[128,128]{1,0:T(8,128)} copy(f32[128,128]{1,0:T(8,128)S(1)} %get-tuple-element.17) | data formatting | bytes 131072
  44.9 0.9 %copy.26 = f32[24,64,128]{2,1,0:T(8,128)} copy(f32[24,64,128]{2,1,0:T(8,128)S(1)} %get-tuple-element.18) | data formatting | bytes 1572864
  45.7 0.6 %copy.27 = f32[24,64]{1,0:T(8,128)} copy(f32[24,64]{1,0:T(8,128)S(1)} %get-tuple-element.19) | data formatting | bytes 12288
  (17 shorter events, 0.1 us)
Async XLA Ops:
  0.7 0.7 %copy-start.5 = (s32[8,2]{0,1:T(2,128)S(1)}, s32[8,2]{0,1:T(2,128)}, u32[]{:S(2)}) copy-start(s32[8,2]{0,1:T(2,128)} %param.9) | copy-start | bytes 196
  1.7 0.7 %copy-start.6 = (s32[8,2]{0,1:T(2,128)S(1)}, s32[8,2]{0,1:T(2,128)}, u32[]{:S(2)}) copy-start(s32[8,2]{0,1:T(2,128)} %param.10) | copy-start | bytes 196
  3.0 0.7 %copy-start.4 = (s32[128]{0:T(128)S(1)}, s32[128]{0:T(128)}, u32[]{:S(2)}) copy-start(s32[128]{0:T(128)} %param.11) | copy-start | bytes 1540
  3.8 0.7 %copy-start.3 = (s32[128,8]{0,1:T(8,128)S(1)}, s32[128,8]{0,1:T(8,128)}, u32[]{:S(2)}) copy-start(s32[128,8]{0,1:T(8,128)} %param.12) | copy-start | bytes 12292
  4.5 0.8 %copy-start.1 = (f32[128,128]{1,0:T(8,128)S(1)}, f32[128,128]{1,0:T(8,128)}, u32[]{:S(2)}) copy-start(f32[128,128]{1,0:T(8,128)} %grad.1) | copy-start | bytes 196612
  4.6 0.7 %copy-start.2 = (f32[24,64]{1,0:T(8,128)S(1)}, f32[24,64]{1,0:T(8,128)}, u32[]{:S(2)}) copy-start(f32[24,64]{1,0:T(8,128)} %accum.1) | copy-start | bytes 18436
  5.4 1.1 %copy-start = (f32[24,64,128]{2,1,0:T(8,128)S(1)}, f32[24,64,128]{2,1,0:T(8,128)}, u32[]{:S(2)}) copy-start(f32[24,64,128]{2,1,0:T(8,128)} %table.1) | copy-start | bytes 2359300

commit v2 on v1

--- a/solution.py
+++ b/solution.py
@@ -296,10 +296,10 @@
 
 def gather_kernel(
     n, reps, cap,
-    picked, source, bucket_col, lane_col, rows_t, named_t, table, accum, grad,
+    dest, slot, bag_block, bag_rows, accum, table, grad,
     pooled_out, table_out, accum_out,
     comb, mig_send, ids_send, units, ids, moved_hl, total, pool_part, pool_back,
-    send_sem, recv_sem, zsend_sem, zrecv_sem, usend_sem, urecv_sem, psend_sem, precv_sem,
+    send_sem, recv_sem, zsend_sem, zrecv_sem, usend_sem, urecv_sem, psend_sem, precv_sem, load_sem, held,
 ):
     me = lax.axis_index("table")
     rep = lax.axis_index("batch")
@@ -327,17 +327,28 @@
     def _():
         pl.semaphore_signal(barrier, inc=1, device_id={"batch": rep - 1}, device_id_type=MESH)
 
-    units[rep, me, 0:samples, :] = grad[...]
-    units[rep, me, samples:, :] = named_t[...]
-    lanes = (
-        lax.broadcasted_iota(jnp.int32, (samples, n * 128), 1) == lane_col[...]
-    ).astype(jnp.float32)
-    sent_ids = jnp.dot(rows_t[...], lanes, precision=EXACT, preferred_element_type=jnp.float32)
-    for d in range(n):
-        ids_send[d] = sent_ids[:, d * 128 : (d + 1) * 128]
-        mig_send[d, 0:brows, :] = table[picked[d]]
-        mig_send[d, brows:, :] = jnp.zeros((8, dim), jnp.float32)
-        mig_send[d, brows : brows + 1, 0:brows] = accum[pl.ds(picked[d], 1), :]
+    load_grad = pltpu.make_async_copy(
+        grad, units.at[rep, me, pl.ds(0, samples)], load_sem.at[0]
+    )
+    load_table = pltpu.make_async_copy(
+        table, comb.at[pl.ds(0, blocks), pl.ds(0, brows)], load_sem.at[1]
+    )
+    load_held = pltpu.make_async_copy(table, held, load_sem.at[2])
+    load_grad.start()
+    load_held.start()
+    load_table.start()
+
+    f32 = jnp.float32
+    unit_eye = lax.broadcasted_iota(jnp.int32, (samples, samples), 0) == lax.broadcasted_iota(
+        jnp.int32, (samples, samples), 1
+    )
+    rows_t = lax.dot_general(
+        bag_rows[...].astype(f32), unit_eye.astype(f32), (((0,), (0,)), ((), ())),
+        precision=EXACT, preferred_element_type=f32,
+    )
+    named_t = (bag_block[...] * brows).astype(f32) + rows_t
+    units[rep, me, samples:, :] = named_t
+    load_grad.wait()
 
     neighbours = jnp.where(has_up, 1, 0) + jnp.where(has_down, 1, 0)
     pl.semaphore_wait(barrier, n - 1 + neighbours)
@@ -429,7 +440,7 @@
     def chosen(places, counts, start):
         return jnp.concatenate(
             [
-                jnp.where(places == start + b, counts, 0.0).astype(jnp.bfloat16)
+                jnp.where(places == former(start + b), counts, 0.0).astype(jnp.bfloat16)
                 for b in range(step_blocks)
             ],
             axis=0,
@@ -444,7 +455,7 @@
     def add_units(origin, which):
         places, counts = joined(
             [
-                count_rows(units[origin, u, samples:, :].astype(jnp.int32) - me * (blocks * brows))
+                count_rows(units[origin, u, samples:, :].astype(jnp.int32))
                 for u in which
             ]
         )
@@ -471,12 +482,71 @@
         add_units(origin, beyond)
 
     over(0, enter)
+
+    moving = dest.shape[1]
+    count = jnp.int32(0)
+    giver = [jnp.int32(0)] * moving
+    given = [jnp.int32(0)] * moving
+    for s in range(n):
+        for k in range(moving):
+            hit = dest[s, k] == me
+            for r in range(moving):
+                now = jnp.logical_and(hit, count == r)
+                giver[r] = jnp.where(now, s, giver[r])
+                given[r] = jnp.where(now, s * blocks + slot[s, k], given[r])
+            count = count + jnp.where(hit, 1, 0)
+    freed = [slot[me, r] for r in range(moving)]
+    towards = [dest[me, r] for r in range(moving)]
+
+    def source(j):
+        at = j
+        for r in range(moving):
+            at = jnp.where(j == freed[r], blocks + giver[r], at)
+        return at
+
+    def former(j):
+        at = me * blocks + j
+        for r in range(moving):
+            at = jnp.where(j == freed[r], given[r], at)
+        return at
+
+    owner = jnp.zeros((1, samples), jnp.int32)
+    for t in range(1, n):
+        owner = owner + (bag_block[...] >= t * blocks).astype(jnp.int32)
+    for s in range(n):
+        for k in range(moving):
+            owner = jnp.where(bag_block[...] == s * blocks + slot[s, k], dest[s, k], owner)
+    owner = owner.astype(f32)
+    owner_col = jnp.sum(jnp.where(unit_eye, owner, 0.0), axis=1, keepdims=True)
+    before = lax.broadcasted_iota(jnp.int32, (samples, samples), 1) < lax.broadcasted_iota(
+        jnp.int32, (samples, samples), 0
+    )
+    within = jnp.sum(
+        jnp.where(jnp.logical_and(owner_col == owner, before), 1.0, 0.0), axis=1, keepdims=True
+    ).astype(jnp.int32)
+    owner_col = owner_col.astype(jnp.int32)
+    bucket_col = owner_col * cap + within
+    lane_col = owner_col * 128 + (me % per_group) * cap + within
+    lanes = (
+        lax.broadcasted_iota(jnp.int32, (samples, n * 128), 1) == lane_col
+    ).astype(f32)
+    sent_ids = jnp.dot(named_t + 1.0, lanes, precision=EXACT, preferred_element_type=f32)
+    for d in range(n):
+        ids_send[d] = sent_ids[:, d * 128 : (d + 1) * 128]
     for peer in peers:
         exchange(0, ids_send.at[peer], ids.at[me], peer).start()
+    load_held.wait()
+    load_table.wait()
+    for d in range(n):
+        picked = jnp.int32(0)
+        for r in range(moving):
+            picked = jnp.where(towards[r] == d, freed[r], picked)
+        mig_send[d, 0:brows, :] = held[picked]
+        mig_send[d, brows:, :] = jnp.zeros((8, dim), f32)
+        mig_send[d, brows : brows + 1, 0:brows] = accum[pl.ds(picked, 1), :]
     for peer in peers:
         exchange(1, mig_send.at[peer], comb.at[blocks + me], peer).start()
     ids[me] = ids_send[me]
-    comb[0:blocks, 0:brows, :] = table[...]
     comb[0:blocks, brows:, :] = jnp.zeros((blocks, 8, dim), jnp.float32)
     comb[blocks + me] = jnp.zeros((brows + 8, dim), jnp.float32)
     for j in range(blocks):
@@ -502,7 +572,7 @@
 
     def copy_moved(j, carry):
         moved_hl[pl.ds(pl.multiple_of(j * brows, brows), brows), :] = split_halves(
-            comb[source[j], 0:brows, :]
+            comb[source(j), 0:brows, :]
         )
         return carry
 
@@ -546,7 +616,7 @@
         where = pl.ds(pl.multiple_of(j * brows, brows), brows)
         both = total[where, :]
         row_grad = both[:, :dim] + both[:, dim:]
-        at = source[j]
+        at = source(j)
         old = comb[at, brows : brows + 1, 0:brows]
         old = jnp.sum(jnp.where(eye, old, 0.0), axis=1, keepdims=True)
         new = old + jnp.mean(row_grad * row_grad, axis=1, keepdims=True)
@@ -559,7 +629,7 @@
     for peer in peers:
         give_back(peer, peer).wait_recv()
     back = (
-        lax.broadcasted_iota(jnp.int32, (samples, slots), 1) == bucket_col[...]
+        lax.broadcasted_iota(jnp.int32, (samples, slots), 1) == bucket_col
     ).astype(jnp.float32)
     pooled_out[...] = jnp.dot(
         back, pool_back[...].reshape(slots, dim), precision=EXACT,
@@ -596,47 +666,6 @@
     moving = plan_dest.shape[1]
     samples, pool = bag_rows.shape
     cap = 4 * samples // n
-    owners = jnp.arange(n, dtype=jnp.int32)
-
-    targets = plan_dest.reshape(-1)
-    sources = jnp.arange(n * moving, dtype=jnp.int32) // moving
-    earlier = (targets[:, None] == targets[None, :]) & (sources[None, :] < sources[:, None])
-    rank = jnp.sum(earlier.astype(jnp.int32), axis=1)
-    landing_at = targets * moving + rank
-    every = jnp.arange(n * moving, dtype=jnp.int32)
-    landing = jnp.sum(
-        jnp.where(landing_at[:, None] == every[None, :], plan_slot.reshape(-1)[None, :], 0), axis=1
-    )
-    old_spot = sources * blocks + plan_slot.reshape(-1)
-    new_spot = targets * blocks + landing
-
-    mine = sources == me
-    picked = jnp.sum(
-        jnp.where(
-            mine[None, :] & (targets[None, :] == owners[:, None]), plan_slot.reshape(-1)[None, :], 0
-        ),
-        axis=1,
-    )
-    spots = me * blocks + jnp.arange(blocks, dtype=jnp.int32)
-    comes = new_spot[None, :] == spots[:, None]
-    source = jnp.where(
-        jnp.any(comes, axis=1),
-        blocks + jnp.sum(jnp.where(comes, sources[None, :], 0), axis=1),
-        jnp.arange(blocks, dtype=jnp.int32),
-    )
-
-    moves = bag_block[:, None] == old_spot[None, :]
-    read = bag_block + jnp.sum(jnp.where(moves, (new_spot - old_spot)[None, :], 0), axis=1)
-    owner = read // blocks
-    order = jnp.arange(samples, dtype=jnp.int32)
-    slot = jnp.sum(
-        ((owner[:, None] == owner[None, :]) & (order[None, :] < order[:, None])).astype(jnp.int32),
-        axis=1,
-    )
-    bucket = owner * cap + slot
-    lane = owner * 128 + (me % (128 // cap)) * cap + slot
-    rows_t = (((read - owner * blocks) * brows)[None, :] + bag_rows.T + 1).astype(jnp.float32)
-
     vmem = pl.BlockSpec(memory_space=pltpu.VMEM)
     smem = pl.BlockSpec(memory_space=pltpu.SMEM)
     slots = n * cap
@@ -648,11 +677,10 @@
     )
     unit_bytes = 4 * (samples + pool) * dim
     if n == 8 and pool == 8 and samples == 128 and n * reps * unit_bytes <= 16 * 1024 * 1024:
-        named_t = ((read * brows)[None, :] + bag_rows.T).astype(f32)
         return pl.pallas_call(
             functools.partial(gather_kernel, n, reps, cap),
             out_shape=out_shape,
-            in_specs=[smem] * 2 + [vmem] * 7,
+            in_specs=[smem] * 2 + [vmem] * 3 + [pl.BlockSpec(memory_space=pl.ANY)] * 2,
             out_specs=(vmem, vmem, vmem),
             scratch_shapes=[
                 pltpu.VMEM((blocks + n, brows + 8, dim), f32),
@@ -672,14 +700,57 @@
                 pltpu.SemaphoreType.DMA((reps, n)),
                 pltpu.SemaphoreType.DMA((n,)),
                 pltpu.SemaphoreType.DMA((n,)),
+                pltpu.SemaphoreType.DMA((3,)),
+                pltpu.VMEM((blocks, brows, dim), f32),
             ],
             compiler_params=pltpu.CompilerParams(
                 collective_id=1, has_side_effects=True, vmem_limit_bytes=48 * 1024 * 1024
             ),
         )(
-            picked, source, bucket[:, None], lane[:, None], rows_t, named_t,
-            table_rows, accum, grad_pooled,
-        )
+            plan_dest, plan_slot, bag_block[None, :], bag_rows, accum, table_rows, grad_pooled,
+        )
+
+    owners = jnp.arange(n, dtype=jnp.int32)
+
+    targets = plan_dest.reshape(-1)
+    sources = jnp.arange(n * moving, dtype=jnp.int32) // moving
+    earlier = (targets[:, None] == targets[None, :]) & (sources[None, :] < sources[:, None])
+    rank = jnp.sum(earlier.astype(jnp.int32), axis=1)
+    landing_at = targets * moving + rank
+    every = jnp.arange(n * moving, dtype=jnp.int32)
+    landing = jnp.sum(
+        jnp.where(landing_at[:, None] == every[None, :], plan_slot.reshape(-1)[None, :], 0), axis=1
+    )
+    old_spot = sources * blocks + plan_slot.reshape(-1)
+    new_spot = targets * blocks + landing
+
+    mine = sources == me
+    picked = jnp.sum(
+        jnp.where(
+            mine[None, :] & (targets[None, :] == owners[:, None]), plan_slot.reshape(-1)[None, :], 0
+        ),
+        axis=1,
+    )
+    spots = me * blocks + jnp.arange(blocks, dtype=jnp.int32)
+    comes = new_spot[None, :] == spots[:, None]
+    source = jnp.where(
+        jnp.any(comes, axis=1),
+        blocks + jnp.sum(jnp.where(comes, sources[None, :], 0), axis=1),
+        jnp.arange(blocks, dtype=jnp.int32),
+    )
+
+    moves = bag_block[:, None] == old_spot[None, :]
+    read = bag_block + jnp.sum(jnp.where(moves, (new_spot - old_spot)[None, :], 0), axis=1)
+    owner = read // blocks
+    order = jnp.arange(samples, dtype=jnp.int32)
+    slot = jnp.sum(
+        ((owner[:, None] == owner[None, :]) & (order[None, :] < order[:, None])).astype(jnp.int32),
+        axis=1,
+    )
+    bucket = owner * cap + slot
+    lane = owner * 128 + (me % (128 // cap)) * cap + slot
+    rows_t = (((read - owner * blocks) * brows)[None, :] + bag_rows.T + 1).astype(jnp.float32)
+
     return pl.pallas_call(
         functools.partial(bucket_kernel, n, reps, cap),
         out_shape=out_shape,

time: 46.6 us -> 44.5 us (0.955)
  local copies, waits for them, and re-layouts: 6.87 us -> 5.6 us
  other arithmetic: 0.99 us -> 0 us
    unnamed x19 -> x14, local copies, waits for them, and re-layouts: 6.49 us -> 5.6 us
    reduce_sum x6 -> x0, other arithmetic: 0.83 us -> none  [the longest x1 0.18 us: per_device(): rank = jnp.sum(earlier.astype(jnp.int32), axis=1)]
where the time goes in v2:
time: 44.5 us; the launch traced here: 44.2 us
  Pallas kernels  38 us (85%)
  local copies, waits for them, and re-layouts  5.6 us (13%)
  between operations  0.68 us (2%)
    pallas_call x1, Pallas kernels, per_device(): pl.pallas_call(functools.partial(gather_kernel, n, reps, cap), out_shape=...  38 us
    unnamed x14, local copies, waits for them, and re-layouts  5.6 us

profile of v2, /device:TPU:0, one launch (start us, length us, event | category | flops | bytes accessed | tf_op | source)
XLA Modules:
  0.0 44.2 jit_solution(12239349604187330960)
XLA Ops:
  0.6 0.0 copy-start.1
  0.6 0.8 %copy.10.dest = s32[8,2]{1,0:T(8,128)S(1)} copy(s32[8,2]{0,1:T(2,128)} %param.9) | data formatting | bytes 128 | tf_op args[2]
  1.4 0.8 %copy.11.slot = s32[8,2]{1,0:T(8,128)S(1)} copy(s32[8,2]{0,1:T(2,128)} %param.10) | data formatting | bytes 128 | tf_op args[3]
  2.2 0.0 copy-start.2
  2.2 0.0 copy-start.3
  2.2 0.8 %copy.12.bag_rows = s32[128,8]{1,0:T(8,128)S(1)} copy(s32[128,8]{0,1:T(8,128)} %param.12) | data formatting | bytes 8192 | tf_op args[5]
  3.0 0.0 copy-done.1
  3.0 0.0 copy-done.2
  3.0 0.0 copy-done.3
  3.0 0.0 copy-start
  3.0 1.1 %copy-done = f32[24,64,128]{2,1,0:T(8,128)S(1)} copy-done((f32[24,64,128]{2,1,0:T(8,128)S(1)}, f32[24,64,128]{2,1,0:T(8,128)}, u32[]{:S(2)}) %copy-start) | copy-done | bytes 786456
  4.2 38.0 %shard_map.94 = (f32[128,128]{1,0:T(8,128)S(1)}, f32[24,64,128]{2,1,0:T(8,128)S(1)}, f32[24,64]{1,0:T(8,128)S(1)}) custom-call(s32[8,2]{1,0:T(8,128)S(1)} %copy.10.dest, s32[8,2]{1,0:T(8,128)S(1)} %copy.11.slot, s32[1,128]{1,0:T(1,128)S(1)} %bitcast.1, s32[128,8]{1,0:T(8,128)S(1)} %copy.12.bag_rows, f32[24,64]{1,0:T(8,128)S(1)} %copy-done.2, ...), custom_call_target="tpu_custom_call" | custom-call | tf_op jit(solution)/shard_map/pallas_call | solution.py:680
  42.1 0.6 %copy.16 = f32[128,128]{1,0:T(8,128)} copy(f32[128,128]{1,0:T(8,128)S(1)} %get-tuple-element.6) | data formatting | bytes 131072
  42.8 0.9 %copy.17 = f32[24,64,128]{2,1,0:T(8,128)} copy(f32[24,64,128]{2,1,0:T(8,128)S(1)} %get-tuple-element.7) | data formatting | bytes 1572864
  43.6 0.6 %copy.18 = f32[24,64]{1,0:T(8,128)} copy(f32[24,64]{1,0:T(8,128)S(1)} %get-tuple-element.8) | data formatting | bytes 12288
Async XLA Ops:
  0.6 2.4 %copy-start.1 = (f32[128,128]{1,0:T(8,128)S(1)}, f32[128,128]{1,0:T(8,128)}, u32[]{:S(2)}) copy-start(f32[128,128]{1,0:T(8,128)} %grad.1) | copy-start | bytes 196612
  2.2 0.8 %copy-start.2 = (f32[24,64]{1,0:T(8,128)S(1)}, f32[24,64]{1,0:T(8,128)}, u32[]{:S(2)}) copy-start(f32[24,64]{1,0:T(8,128)} %accum.1) | copy-start | bytes 18436
  2.2 0.8 %copy-start.3 = (s32[128]{0:T(128)S(1)}, s32[128]{0:T(128)}, u32[]{:S(2)}) copy-start(s32[128]{0:T(128)} %param.11) | copy-start | bytes 1540
  3.0 1.1 %copy-start = (f32[24,64,128]{2,1,0:T(8,128)S(1)}, f32[24,64,128]{2,1,0:T(8,128)}, u32[]{:S(2)}) copy-start(f32[24,64,128]{2,1,0:T(8,128)} %table.1) | copy-start | bytes 2359300

commit v3 on v2

--- a/solution.py
+++ b/solution.py
@@ -471,15 +471,12 @@
 
         lax.fori_loop(0, blocks // step_blocks, step, 0)
 
-    def finish_near(origin, way):
-        add_units(origin, (me, first, second, corner))
-
     beyond = [u + 1 - 2 * parity for u in (me, first, second, corner)]
 
-    def finish_far(origin, way):
+    def finish(origin, way):
         for unit in beyond:
             relay(2, origin, unit).wait_recv()
-        add_units(origin, beyond)
+        add_units(origin, [me, first, second, corner] + beyond)
 
     over(0, enter)
 
@@ -604,7 +601,7 @@
         for lag, body in ((0, enter), (1, from_first), (2, from_second)):
             if 0 <= step - lag < reps:
                 over(step - lag, body)
-        for lag, body in ((2, finish_near), (3, finish_far)):
+        for lag, body in ((3, finish),):
             if 0 <= step - lag < reps:
                 over(step - lag, body)
 

time: 44.5 us -> 42.7 us (0.960)
  Pallas kernels: 38 us -> 36.2 us
    pallas_call x1, Pallas kernels: 38 us -> 36.2 us  [per_device(): pl.pallas_call(functools.partial(gather_kernel, n, reps, cap), out_shape=...]
where the time goes in v3:
time: 42.7 us; the launch traced here: 42.5 us
  Pallas kernels  36.2 us (85%)
  local copies, waits for them, and re-layouts  5.6 us (13%)
  between operations  0.68 us (2%)
    pallas_call x1, Pallas kernels, per_device(): pl.pallas_call(functools.partial(gather_kernel, n, reps, cap), out_shape=...  36.2 us
    unnamed x14, local copies, waits for them, and re-layouts  5.6 us

profile of v3, /device:TPU:0, one launch (start us, length us, event | category | flops | bytes accessed | tf_op | source)
XLA Modules:
  0.0 42.5 jit_solution(17743703940145773175)
XLA Ops:
  0.6 0.0 copy-start.1
  0.6 0.8 %copy.10.dest = s32[8,2]{1,0:T(8,128)S(1)} copy(s32[8,2]{0,1:T(2,128)} %param.9) | data formatting | bytes 128 | tf_op args[2]
  1.4 0.8 %copy.11.slot = s32[8,2]{1,0:T(8,128)S(1)} copy(s32[8,2]{0,1:T(2,128)} %param.10) | data formatting | bytes 128 | tf_op args[3]
  2.2 0.0 copy-start.2
  2.2 0.0 copy-start.3
  2.2 0.8 %copy.12.bag_rows = s32[128,8]{1,0:T(8,128)S(1)} copy(s32[128,8]{0,1:T(8,128)} %param.12) | data formatting | bytes 8192 | tf_op args[5]
  3.0 0.0 copy-done.1
  3.0 0.0 copy-done.2
  3.0 0.0 copy-done.3
  3.0 0.0 copy-start
  3.0 1.1 %copy-done = f32[24,64,128]{2,1,0:T(8,128)S(1)} copy-done((f32[24,64,128]{2,1,0:T(8,128)S(1)}, f32[24,64,128]{2,1,0:T(8,128)}, u32[]{:S(2)}) %copy-start) | copy-done | bytes 786456
  4.2 36.2 %shard_map.94 = (f32[128,128]{1,0:T(8,128)S(1)}, f32[24,64,128]{2,1,0:T(8,128)S(1)}, f32[24,64]{1,0:T(8,128)S(1)}) custom-call(s32[8,2]{1,0:T(8,128)S(1)} %copy.10.dest, s32[8,2]{1,0:T(8,128)S(1)} %copy.11.slot, s32[1,128]{1,0:T(1,128)S(1)} %bitcast.1, s32[128,8]{1,0:T(8,128)S(1)} %copy.12.bag_rows, f32[24,64]{1,0:T(8,128)S(1)} %copy-done.2, ...), custom_call_target="tpu_custom_call" | custom-call | tf_op jit(solution)/shard_map/pallas_call | solution.py:677
  40.3 0.6 %copy.16 = f32[128,128]{1,0:T(8,128)} copy(f32[128,128]{1,0:T(8,128)S(1)} %get-tuple-element.6) | data formatting | bytes 131072
  41.0 0.9 %copy.17 = f32[24,64,128]{2,1,0:T(8,128)} copy(f32[24,64,128]{2,1,0:T(8,128)S(1)} %get-tuple-element.7) | data formatting | bytes 1572864
  41.9 0.6 %copy.18 = f32[24,64]{1,0:T(8,128)} copy(f32[24,64]{1,0:T(8,128)S(1)} %get-tuple-element.8) | data formatting | bytes 12288
Async XLA Ops:
  0.6 2.4 %copy-start.1 = (f32[128,128]{1,0:T(8,128)S(1)}, f32[128,128]{1,0:T(8,128)}, u32[]{:S(2)}) copy-start(f32[128,128]{1,0:T(8,128)} %grad.1) | copy-start | bytes 196612
  2.2 0.8 %copy-start.2 = (f32[24,64]{1,0:T(8,128)S(1)}, f32[24,64]{1,0:T(8,128)}, u32[]{:S(2)}) copy-start(f32[24,64]{1,0:T(8,128)} %accum.1) | copy-start | bytes 18436
  2.2 0.8 %copy-start.3 = (s32[128]{0:T(128)S(1)}, s32[128]{0:T(128)}, u32[]{:S(2)}) copy-start(s32[128]{0:T(128)} %param.11) | copy-start | bytes 1540
  3.0 1.1 %copy-start = (f32[24,64,128]{2,1,0:T(8,128)S(1)}, f32[24,64,128]{2,1,0:T(8,128)}, u32[]{:S(2)}) copy-start(f32[24,64,128]{2,1,0:T(8,128)} %table.1) | copy-start | bytes 2359300
